TPU v7x, 256 devices: a whole 4x4x8 slice. The times are simulated.
256 devices in a mesh: seg: 32 (over x, z), term: 8 (over y, core).
Axes of the slice: x: 4, y: 4, z: 8, core: 2. Of those that a mesh axis runs over, the one named last changes fastest.
Arguments:
- left_blocks: bfloat16 [32, 32, 512, 512], P('seg', 'term'), may hold values from -0.25 to 0.25
- right_blocks: bfloat16 [32, 32, 512, 512], P('seg', 'term'), may hold values from -0.046875 to 0.046875
- start_state: float32 [32, 512, 512], P('seg'), may hold values from -6 to 6
- left_transfer: float32 [32, 512, 512], P('seg'), as said below
- right_transfer: float32 [32, 512, 512], P('seg'), as said below
- ranks: int32 [32, 2], P('seg'), may hold values from 128 to 512
Outputs:
- final_state: float32 [32, 512, 512], P('seg')
Inputs may be any that keep to these rules, and one draw needn't show every extreme that they name: `left_transfer`: entries of size about 0.3 / sqrt(512). `right_transfer`: entries of size about 0.3 / sqrt(512).
All inputs are finite; a program needn't handle non-finite values.
Results may differ from a plain program's by a relative error of at most 0.008.
Values may be sent and summed in bfloat16 or wider, within the bound.
A program may use at most 128 MiB of HBM per device.

v0:
```python
import jax
import jax.numpy as jnp
from jax import lax
from jax.sharding import PartitionSpec as P

ITERS = 2


def prefix(part, axis, combine, identity, reverse):
    count = lax.axis_size(axis)
    place = lax.axis_index(axis)
    ahead = count - 1 - place if reverse else place
    gathered = lax.all_gather(part, axis)
    state = jnp.zeros_like(part) + jnp.asarray(identity, part.dtype)

    def one(lap, state):
        source = count - 1 - lap if reverse else lap
        return combine(state, lax.dynamic_index_in_dim(gathered, source, 0, False))

    return lax.fori_loop(0, ahead, one, state)


def passed_along(shard, axis, by):
    length = lax.axis_size(axis)
    pairs = [(i, i + by) for i in range(length) if 0 <= i + by < length]
    return lax.ppermute(shard, axis, pairs)


def normed(block, target):
    return block * (target / jnp.sqrt(jnp.sum(block * block) + 1e-06))


def combine_env(earlier, later):
    root = float(earlier.shape[0]) ** 0.5
    return normed(jnp.dot(earlier, later, precision=lax.Precision.HIGHEST), root)


def term_partial(left_ops, right_ops, moved):
    inner = jnp.einsum("tij,jk->tik", left_ops, moved, preferred_element_type=jnp.float32).astype(
        jnp.bfloat16
    )
    return jnp.einsum("tik,tlk->il", inner, right_ops, preferred_element_type=jnp.float32)


def half_sweep(left_ops, right_ops, basis, start, live_mask):
    block_size = start.shape[0]
    basis_b = basis.astype(jnp.bfloat16)
    basis_wide = basis_b.astype(jnp.float32)
    state = normed(start * live_mask, float(block_size))
    for step_index in range(ITERS):
        state_b = state.astype(jnp.bfloat16)
        moved = jnp.dot(basis_b, state_b, preferred_element_type=jnp.float32).astype(jnp.bfloat16)
        partial_sum = term_partial(left_ops, right_ops, moved)
        term_total = lax.psum(partial_sum, "term")
        applied = lax.dot_general(
            basis_wide, term_total, (((0,), (0,)), ((), ())), precision=lax.Precision.HIGHEST
        )
        state = normed((2.0 * state - applied) * live_mask, float(block_size))
    return state


def per_device(left_blocks, right_blocks, start_state, left_transfer, right_transfer, ranks):
    block_size = start_state.shape[-1]
    unit_matrix = jnp.eye(block_size, dtype=jnp.float32)
    root = float(block_size) ** 0.5
    left_unit = normed(unit_matrix + left_transfer[0], root)
    right_unit = normed(unit_matrix + right_transfer[0], root)
    left_env = prefix(left_unit, "seg", combine_env, unit_matrix, False)
    right_env = prefix(right_unit, "seg", combine_env, unit_matrix, True)
    positions = jnp.arange(block_size)
    rows_live = (positions < ranks[0, 0]).astype(jnp.float32)
    cols_live = (positions < ranks[0, 1]).astype(jnp.float32)
    live_mask = rows_live[:, None] * cols_live[None, :]
    first_state = half_sweep(left_blocks[0], right_blocks[0], left_env, start_state[0], live_mask)
    neighbour = passed_along(first_state.astype(jnp.bfloat16), "seg", 1)
    seeded = first_state + 0.5 * neighbour.astype(jnp.float32)
    flipped = half_sweep(right_blocks[0], left_blocks[0], right_env.T, seeded.T, live_mask.T)
    return flipped.T[None]


def solution(mesh):
    in_specs = (
        P("seg", "term", None, None),
        P("seg", "term", None, None),
        P("seg", None, None),
        P("seg", None, None),
        P("seg", None, None),
        P("seg", None),
    )
    out_specs = P("seg", None, None)
    return jax.shard_map(
        per_device, mesh=mesh, in_specs=in_specs, out_specs=out_specs, check_vma=False
    )
```

profile of v0, /device:TPU:1, one launch (start us, length us, event | category | flops | bytes accessed | tf_op | source)
XLA Modules:
  0.0 1194.9 jit_solution(1782328151539934472)
XLA Ops:
  20.8 229.4 %all-gather.3.cloned.1.call-done = f32[32,512,512]{2,1,0:T(8,128)} async-done(((f32[1,512,512]{2,1,0:T(8,128)}), f32[32,512,512]{2,1,0:T(8,128)}) %all-gather.3.cloned.1.call-update) | async-done | bytes 33554448 | tf_op jit(solution)/shard_map/all_gather | solution.py:13
  251.4 5.2 fusion.28
  268.2 237.8 %all-reduce.5.cloned.1.call-done = f32[512,512]{1,0:T(8,128)} async-done(((f32[512,512]{1,0:T(8,128)}), f32[512,512]{1,0:T(8,128)}) %all-reduce.5.cloned.1.call-update) | async-done | bytes 1048592 | tf_op jit(solution)/shard_map/psum | solution.py:54
  506.0 4.4 multiply_reduce_fusion.5
  511.1 5.1 fusion.31
  529.8 59.2 %all-reduce.7.cloned.1.call-done = f32[512,512]{1,0:T(8,128)} async-done(((f32[512,512]{1,0:T(8,128)}), f32[512,512]{1,0:T(8,128)}) %all-reduce.7.cloned.1.call-update) | async-done | bytes 1048592 | tf_op jit(solution)/shard_map/psum | solution.py:54
  588.9 4.4 multiply_reduce_fusion.4
  596.2 4.0 collective-permute-start
  600.1 230.8 %all-gather.5.cloned.1.call-done = f32[32,512,512]{2,1,0:T(8,128)} async-done(((f32[1,512,512]{2,1,0:T(8,128)}), f32[32,512,512]{2,1,0:T(8,128)}) %all-gather.5.cloned.1.call-update) | async-done | bytes 33554448 | tf_op jit(solution)/shard_map/all_gather | solution.py:13
  831.0 180.6 %while.23 = (s32[]{:T(128)}, f32[512,512]{0,1:T(8,128)}, s32[]{:T(128)}, f32[32,512,512]{2,1,0:T(8,128)}, s32[]{:T(128)}, /*index=5*/s32[]{:T(128)}, s32[]{:T(128)}, s32[]{:T(128)}, f32[]{:T(128)}, f32[]{:T(128)}) while((s32[]{:T(128)}, f32[512,512]{0,1:T(8,128)}, s32[]{:T(128)}, f32[32,512,512]{2,1,0:T(8,128)}, s32[]{:T(128)}, ...), condition=%wide.region_13.14_spmd, body=%wide.region_11.13_spmd.sunk | while | flops 1611399168 | bytes 5243071 | solution.py:20
  831.0 4.1 multiply_reduce_fusion.10
  836.8 4.1 multiply_reduce_fusion.10
  842.6 4.1 multiply_reduce_fusion.10
  848.4 4.1 multiply_reduce_fusion.10
  854.3 4.1 multiply_reduce_fusion.10
  860.1 4.1 multiply_reduce_fusion.10
  865.9 4.1 multiply_reduce_fusion.10
  871.7 4.1 multiply_reduce_fusion.10
  877.6 4.1 multiply_reduce_fusion.10
  883.4 4.1 multiply_reduce_fusion.10
  889.2 4.1 multiply_reduce_fusion.10
  895.0 4.1 multiply_reduce_fusion.10
  900.9 4.1 multiply_reduce_fusion.10
  906.7 4.1 multiply_reduce_fusion.10
  912.5 4.1 multiply_reduce_fusion.10
  918.3 4.1 multiply_reduce_fusion.10
  924.2 4.1 multiply_reduce_fusion.10
  930.0 4.1 multiply_reduce_fusion.10
  935.8 4.1 multiply_reduce_fusion.10
  941.6 4.1 multiply_reduce_fusion.10
  947.5 4.1 multiply_reduce_fusion.10
  953.3 4.1 multiply_reduce_fusion.10
  959.1 4.1 multiply_reduce_fusion.10
  964.9 4.1 multiply_reduce_fusion.10
  970.8 4.1 multiply_reduce_fusion.10
  976.6 4.1 multiply_reduce_fusion.10
  982.4 4.1 multiply_reduce_fusion.10
  988.2 4.1 multiply_reduce_fusion.10
  994.0 4.1 multiply_reduce_fusion.10
  999.9 4.1 multiply_reduce_fusion.10
  1005.7 4.1 multiply_reduce_fusion.10
  1016.5 4.2 fusion.34
  1020.6 3.4 copy.62
  1026.4 59.7 %all-reduce.9.cloned.1.call-done = f32[512,512]{1,0:T(8,128)} async-done(((f32[512,512]{1,0:T(8,128)}), f32[512,512]{1,0:T(8,128)}) %all-reduce.9.cloned.1.call-update) | async-done | bytes 1048592 | tf_op jit(solution)/shard_map/psum | solution.py:54
  1086.1 3.4 fusion.102
  1096.0 4.4 fusion.37
  1107.4 65.8 %all-reduce.11.cloned.1.call-done = f32[512,512]{1,0:T(8,128)} async-done(((f32[512,512]{1,0:T(8,128)}), f32[512,512]{1,0:T(8,128)}) %all-reduce.11.cloned.1.call-update) | async-done | bytes 1048592 | tf_op jit(solution)/shard_map/psum | solution.py:54
  1173.2 3.5 fusion.103
  (100 shorter events, 103.7 us)
Async XLA Ops:
  6.5 253.3 %copy-start = (bf16[1,4,512,512]{3,2,1,0:T(8,128)(2,1)S(1)}, bf16[1,4,512,512]{3,2,1,0:T(8,128)(2,1)}, u32[]{:S(2)}) copy-start(bf16[1,4,512,512]{3,2,1,0:T(8,128)(2,1)} %param.11) | copy-start | bytes 6291460
  6.5 5.6 copy-start.7
  6.5 243.6 %all-gather.3.cloned.1.call-start = ((), (), s32[]{:S(2)}) async-start(), calls=%async_computation | async-start | bytes 34603008 | tf_op jit(solution)/shard_map/all_gather | solution.py:13
  13.3 1.6 copy-start.8
  13.3 492.7 %all-reduce.5.cloned.1.call-start = ((), (), s32[]{:S(2)}) async-start(), calls=%async_computation.1 | async-start | bytes 2097152 | tf_op jit(solution)/shard_map/psum | solution.py:54
  14.9 5.8 copy-start.3
  18.8 1.0 copy-start.1
  251.4 5.2 copy-start.6
  259.9 2.6 copy-start.4
  262.3 326.7 %all-reduce.7.cloned.1.call-start = ((), (), s32[]{:S(2)}) async-start(), calls=%async_computation.2 | async-start | bytes 2097152 | tf_op jit(solution)/shard_map/psum | solution.py:54
  521.8 309.1 %all-gather.5.cloned.1.call-start = ((), (), s32[]{:S(2)}) async-start(), calls=%async_computation.3 | async-start | bytes 34603008 | tf_op jit(solution)/shard_map/all_gather | solution.py:13
  529.7 556.4 %all-reduce.9.cloned.1.call-start = ((), (), s32[]{:S(2)}) async-start(), calls=%async_computation.4 | async-start | bytes 2097152 | tf_op jit(solution)/shard_map/psum | solution.py:54
  596.2 417.5 %collective-permute-start = (bf16[512,512]{1,0:T(8,128)(2,1)}, bf16[512,512]{1,0:T(8,128)(2,1)}, u32[]{:S(2)}, u32[]{:S(2)}) collective-permute-start(bf16[512,512]{1,0:T(8,128)(2,1)} %multiply_convert_fusion.2), channel_id=1, source_target_pairs={{0,8},{8,16},{16,24},{24,32},{32,40},{40,48},{48,56},{56,64},{64,7... | collective-permute-start | bytes 1572872 | tf_op jit(solution)/shard_map/ppermute | solution.py:26
  1011.5 2.2 copy-start.2
  1020.6 3.4 copy-start.9
  1026.3 146.9 %all-reduce.11.cloned.1.call-start = ((), (), s32[]{:S(2)}) async-start(), calls=%async_computation.5 | async-start | bytes 2097152 | tf_op jit(solution)/shard_map/psum | solution.py:54
  1100.4 3.4 copy-start.10
  1176.7 5.9 copy-start.5
Sparse Core Ops, SparseCore 0:
  13.4 236.6 all-gather.2
  262.4 243.5 all-reduce.4
  521.9 66.9 all-reduce.6
  591.4 239.5 all-gather.4
  1026.4 59.5 all-reduce.8
  1106.2 66.9 all-reduce.10
where the time goes:
time: 1200 us; the launch traced here: 1190 us
  waiting for transfers between devices  883 us (74%)
  matrix products  172 us (14%)
  other arithmetic  61.5 us (5%)
  local copies, waits for them, and re-layouts  35.8 us (3%)
  between operations  19.3 us (2%)
  loops' own time  19.2 us (2%)
    all_gather x2, waiting for transfers between devices, prefix(): gathered = lax.all_gather(part, axis)  460 us
    psum x4, waiting for transfers between devices, half_sweep(): term_total = lax.psum(partial_sum, 'term')  422 us
    dot_general x31, matrix products, combine_env(): jnp.dot(earlier, later, precision=lax.Precision.HIGHEST)  128 us
    mul x33, other arithmetic, normed(): return block * (target / jnp.sqrt(jnp.sum(block * block) + 1e-06))  36.8 us
  transfers between devices with their start and end apart: 7, of which 6 were waited for; matrix products, arithmetic and copies ran while one was open for 16% of the time, Pallas kernels for 0%

commit v1 on v0

v1 whole, which is shorter than its diff:
```python
import functools

import jax
import jax.numpy as jnp
from jax import lax
from jax.experimental import pallas as pl
from jax.experimental.pallas import tpu as pltpu
from jax.sharding import PartitionSpec as P

MESH = pl.DeviceIdType.MESH
BF = jnp.bfloat16
F32 = jnp.float32
EPS = 1e-06
ITERS = 2
NY = 4


def dot_ab(a, b):
    return jnp.dot(a, b, preferred_element_type=F32)


def dot_abt(a, b):
    return lax.dot_general(a, b, (((1,), (1,)), ((), ())), preferred_element_type=F32)


def kernel(
    nseg, blk, terms,
    left_hbm, right_hbm, start_hbm, lt_hbm, rt_hbm, ranks, out_ref,
    ops, tr, st, unit, hop, win, env, env_scale, gath, inner, own, s1_out, s1_in, s2_out, s2_in,
    state, part, state_all, part_all, near_out, near_in,
    in_sem, hop_ss, hop_rs, win_ss, win_rs, env_ss, env_rs, gath_ss, gath_rs, all_ss, all_rs, sum_ss, sum_rs,
    s1_sem, s2_ss, s2_rs, near_sem,
):
    levels = nseg.bit_length() - 1
    seg, term = lax.axis_index("seg"), lax.axis_index("term")
    y, core = lax.div(term, 2), lax.rem(term, 2)
    sign = 1 - 2 * core
    place = jnp.where(core == 0, seg, nseg - 1 - seg)
    half, wide, slim = blk // 2, blk // NY, blk // (2 * NY)
    buddy = (seg, term + sign)

    def along(by):
        return (lax.rem(seg + sign * by + 2 * nseg, nseg), term)

    def chip(by):
        return (seg, lax.rem(y + by, NY) * 2 + core)

    def rows(index, size):
        return pl.ds(pl.multiple_of(index * size, size), size)

    def remote(src, dst, ss, rs, to):
        return pltpu.make_async_remote_copy(
            src_ref=src, dst_ref=dst, send_sem=ss, recv_sem=rs, device_id=to, device_id_type=MESH
        )

    load_l = pltpu.make_async_copy(left_hbm.at[0], ops.at[0], in_sem.at[0])
    load_r = pltpu.make_async_copy(right_hbm.at[0], ops.at[1], in_sem.at[1])
    load_s = pltpu.make_async_copy(start_hbm.at[0], st, in_sem.at[2])
    load_lt = pltpu.make_async_copy(lt_hbm.at[0], tr, in_sem.at[3])
    load_rt = pltpu.make_async_copy(rt_hbm.at[0], tr, in_sem.at[3])

    @pl.when(core == 0)
    def _():
        load_lt.start()

    @pl.when(core == 1)
    def _():
        load_rt.start()

    load_s.start()
    load_l.start()
    load_r.start()

    barrier = pltpu.get_barrier_semaphore()
    partners = [chip(1), chip(2), chip(3), buddy]
    for k in range(levels):
        partners.append(along(1 << k))
        if (1 << k) * 2 != nseg:
            partners.append(along(-(1 << k)))
    for to in partners:
        pl.semaphore_signal(barrier, inc=1, device_id=to, device_id_type=MESH)
    load_lt.wait()

    root = float(blk) ** 0.5
    at_row = lax.broadcasted_iota(jnp.int32, (slim, blk), 0)
    at_col = lax.broadcasted_iota(jnp.int32, (slim, blk), 1)

    def set_unit(i, _):
        unit[rows(i, slim), :] = tr[rows(i, slim), :].astype(BF)
        return 0

    lax.fori_loop(0, 2 * NY, set_unit, 0)
    pl.semaphore_wait(barrier, len(partners))

    mine = rows(y, wide)

    def came(slot, distance):
        got = hop[slot]
        return jnp.where(place < distance, jnp.zeros_like(got), got)

    step = remote(unit.at[mine], hop.at[0], hop_ss.at[0], hop_rs.at[0], along(1))
    step.start()
    step.wait_recv()
    a = came(0, 1)
    rest_rows = tr[mine, :] + a.astype(F32) + dot_ab(a, unit[...])
    win[0, mine, :] = rest_rows.astype(BF)
    step.wait_send()

    for k in range(1, levels):
        w = win.at[k - 1]
        step = remote(w.at[mine], hop.at[k], hop_ss.at[k], hop_rs.at[k], along(1 << k))
        spread = [
            remote(w.at[mine], w.at[mine], win_ss.at[k - 1, i], win_rs.at[k - 1, i], chip(i + 1))
            for i in range(3)
        ]
        step.start()
        for s in spread:
            s.start()
        step.wait_recv()
        for s in spread:
            s.wait_recv()
        a = came(k, 1 << k)
        rest_rows = rest_rows + a.astype(F32) + dot_ab(a, win[k - 1])
        win[k, mine, :] = rest_rows.astype(BF)
        step.wait_send()
        for s in spread:
            s.wait_send()

    last = levels - 1
    step = remote(win.at[last, mine], hop.at[levels], hop_ss.at[levels], hop_rs.at[levels], along(1))
    step.start()
    step.wait_recv()
    eye_rows = jnp.where(
        lax.broadcasted_iota(jnp.int32, (wide, blk), 0) + y * wide
        == lax.broadcasted_iota(jnp.int32, (wide, blk), 1),
        1.0, 0.0,
    )
    env[core, mine, :] = (eye_rows + came(levels, 1).astype(F32)).astype(BF)
    step.wait_send()

    def fold(load, combine, start):
        def one(i, acc):
            return combine(acc, load(i).reshape(slim // 8, 8, blk))

        return lax.fori_loop(0, 2 * NY, one, jnp.full((8, blk), start, F32))

    def square_sum(load):
        acc = fold(load, lambda acc, v: acc + jnp.sum(v * v, axis=0), 0.0)
        return jnp.sum(acc, axis=(0, 1), keepdims=True)

    def largest(load):
        acc = fold(load, lambda acc, v: jnp.maximum(acc, jnp.max(jnp.abs(v), axis=0)), 0.0)
        return jnp.max(acc, axis=(0, 1), keepdims=True)

    def spread_out(view, ss, rs):
        own_view = view(core, y)
        out = [remote(own_view, own_view, ss.at[i], rs.at[i], chip(i + 1)) for i in range(3)]
        out.append(remote(own_view, own_view, ss.at[3], rs.at[3], buddy))
        for o in out:
            o.start()
        return out

    def pass_on(view, out, ss, rs):
        for i in range(3):
            got = view(core, lax.rem(y + NY - 1 - i, NY))
            out[i].wait_recv()
            fwd = remote(got, got, ss.at[4 + i], rs.at[4 + i], buddy)
            fwd.start()
            out.append(fwd)

    def rest(out):
        for o in out[3:]:
            o.wait_recv()

    def sent(out):
        for o in out:
            o.wait_send()

    env_view = lambda c, yy: env.at[c, rows(yy, wide)]
    out = spread_out(env_view, env_ss, env_rs)
    pass_on(env_view, out, env_ss, env_rs)
    rest(out)
    for h in range(2):
        env_rows = lambda i: env[h, rows(i, slim), :].astype(F32)
        down = 1.0 / jnp.maximum(largest(env_rows), 1e-30)
        norm = down * (root / jnp.sqrt(square_sum(lambda i: env_rows(i) * down) + EPS))
        env_scale[h] = jnp.broadcast_to(norm, (8, 128))
    sent(out)

    slot = core * NY + y
    my_rows = rows(slot, slim)
    other = rows(1 - core, half)
    ours = rows(core, half)

    def masked(x, low, high):
        live = (at_row + slot * slim < low) & (at_col < high)
        return jnp.where(live, x, 0.0)

    def note(line, x):
        part[pl.ds(line, 1), :] = jnp.broadcast_to(jnp.sum(x * x, axis=(0, 1), keepdims=True), (1, 128))

    load_s.wait()
    rank0, rank1 = ranks[0, 0], ranks[0, 1]

    def live_start(i):
        v = st[rows(i, slim), :]
        return jnp.where((at_row + i * slim < rank0) & (at_col < rank1), v, 0.0)

    scale = float(blk) / jnp.sqrt(square_sum(live_start) + EPS)
    tr[...] = jnp.transpose(st[...])
    state[...] = masked(tr[my_rows, :], rank1, rank0) * scale
    part[...] = jnp.zeros((8, 128), F32)
    load_l.wait()
    load_r.wait()

    gath_view = lambda c, yy: gath.at[rows(c * NY + yy, slim)]
    all_view = lambda c, yy: state_all.at[rows(c * NY + yy, slim)]
    sum_view = lambda c, yy: part_all.at[c * NY + yy]

    def collect():
        state_all[my_rows, :] = state[...].astype(BF)
        part_all[slot] = part[...]
        sums = spread_out(sum_view, sum_ss, sum_rs)
        full = spread_out(all_view, all_ss, all_rs)
        pass_on(sum_view, sums, sum_ss, sum_rs)
        pass_on(all_view, full, all_ss, all_rs)
        rest(sums)
        rest(full)
        total = part_all[0]
        for i in range(1, 2 * NY):
            total = total + part_all[i]
        sent(sums)
        sent(full)
        return total

    def overall(total, scale):
        for line in range(1, ITERS + 1):
            s = total[line : line + 1, 0:1]
            scale = scale * (float(blk) / jnp.sqrt(scale * scale * s + EPS))
        return scale

    def turn():
        total = collect()
        scale = overall(total, jnp.ones((1, 1), F32))
        pick = jnp.where(at_row + slot * slim == at_col, 1.0, 0.0).astype(BF)
        first = dot_abt(pick, state_all[...]) * scale
        near_out[...] = first.astype(BF)
        to = (lax.rem(seg + 1, nseg), term)
        step = remote(near_out, near_in, near_sem.at[0], near_sem.at[1], to)
        step.start()
        step.wait()
        near = jnp.where(seg > 0, near_in[...].astype(F32), 0.0)
        x = masked(first + 0.5 * near, rank0, rank1)
        state[...] = x
        note(0, x)

    def iteration(n, _):
        h = lax.div(n, ITERS)
        gain = env_scale[h, 0:1, 0:1]

        @pl.when(n == ITERS)
        def _():
            turn()

        x = state[...].astype(BF)

        @pl.when(h == 0)
        def _():
            gath[my_rows, :] = (dot_abt(x, env[0]) * gain).astype(BF)

        @pl.when(h == 1)
        def _():
            gath[my_rows, :] = (dot_ab(x, env[1]) * gain).astype(BF)

        out = spread_out(gath_view, gath_ss, gath_rs)
        pass_on(gath_view, out, gath_ss, gath_rs)

        def apply_first(at):
            def one(w, _):
                inner[w, at, :] = dot_abt(gath[at, :], ops[h, w]).astype(BF)
                return 0

            lax.fori_loop(0, terms, one, 0)

        apply_first(ours)
        rest(out)
        apply_first(other)

        def apply_second(at):
            acc = dot_ab(ops[1 - h, 0, at, :], inner[0])
            for w in range(1, terms):
                acc = acc + dot_ab(ops[1 - h, w, at, :], inner[w])
            return acc

        s1_out[...] = apply_second(other).astype(BF)
        pair = remote(s1_out, s1_in, s1_sem.at[0], s1_sem.at[1], buddy)
        pair.start()
        own[...] = apply_second(ours)
        sent(out)
        pair.wait_recv()
        own[...] += s1_in[...].astype(F32)
        pieces = []
        for i in range(3):
            to = lax.rem(y + 1 + i, NY)
            s2_out[i] = own[rows(to, slim), :].astype(BF)
            piece = remote(s2_out.at[i], s2_in.at[i], s2_ss.at[i], s2_rs.at[i], chip(i + 1))
            piece.start()
            pieces.append(piece)
        total = own[rows(y, slim), :]
        for i in range(3):
            pieces[i].wait_recv()
            total = total + s2_in[i].astype(F32)
        high = total.astype(BF)

        def advance(applied):
            live_row = jnp.where(h == 0, rank1, rank0)
            live_col = jnp.where(h == 0, rank0, rank1)
            x = masked(2.0 * state[...] - applied * gain, live_row, live_col)
            state[...] = x
            note(1 + n - h * ITERS, x)

        @pl.when(h == 0)
        def _():
            advance(dot_ab(high, env[0]))

        @pl.when(h == 1)
        def _():
            advance(dot_abt(high, env[1]))

        pair.wait_send()
        for piece in pieces:
            piece.wait_send()
        return 0

    lax.fori_loop(0, 2 * ITERS, iteration, 0)
    total = collect()
    scale = overall(total, float(blk) / jnp.sqrt(total[0:1, 0:1] + EPS))
    out_ref[...] = state_all[...].astype(F32) * scale


def per_device(nseg, left_blocks, right_blocks, start_state, left_transfer, right_transfer, ranks):
    blk, terms = left_blocks.shape[-1], left_blocks.shape[1]
    levels = nseg.bit_length() - 1
    half, wide, slim = blk // 2, blk // NY, blk // (2 * NY)
    dma = pltpu.SemaphoreType.DMA
    scratch = [
        pltpu.VMEM((2, terms, blk, blk), BF),
        pltpu.VMEM((blk, blk), F32),
        pltpu.VMEM((blk, blk), F32),
        pltpu.VMEM((blk, blk), BF),
        pltpu.VMEM((levels + 1, wide, blk), BF),
        pltpu.VMEM((levels, blk, blk), BF),
        pltpu.VMEM((2, blk, blk), BF),
        pltpu.VMEM((2, 8, 128), F32),
        pltpu.VMEM((blk, blk), BF),
        pltpu.VMEM((terms, blk, blk), BF),
        pltpu.VMEM((half, blk), F32),
        pltpu.VMEM((half, blk), BF),
        pltpu.VMEM((half, blk), BF),
        pltpu.VMEM((3, slim, blk), BF),
        pltpu.VMEM((3, slim, blk), BF),
        pltpu.VMEM((slim, blk), F32),
        pltpu.VMEM((8, 128), F32),
        pltpu.VMEM((blk, blk), BF),
        pltpu.VMEM((2 * NY, 8, 128), F32),
        pltpu.VMEM((slim, blk), BF),
        pltpu.VMEM((slim, blk), BF),
        dma((4,)),
        dma((levels + 1,)), dma((levels + 1,)),
        dma((levels, 3)), dma((levels, 3)),
        dma((7,)), dma((7,)),
        dma((7,)), dma((7,)),
        dma((7,)), dma((7,)),
        dma((7,)), dma((7,)),
        dma((2,)),
        dma((3,)), dma((3,)),
        dma((2,)),
    ]
    any_space = pl.BlockSpec(memory_space=pl.ANY)
    final = pl.pallas_call(
        functools.partial(kernel, nseg, blk, terms),
        out_shape=jax.ShapeDtypeStruct((blk, blk), F32),
        in_specs=[any_space] * 5 + [pl.BlockSpec(memory_space=pltpu.SMEM)],
        out_specs=pl.BlockSpec(memory_space=pltpu.VMEM),
        scratch_shapes=scratch,
        compiler_params=pltpu.CompilerParams(
            collective_id=0, has_side_effects=True, vmem_limit_bytes=48 * 1024 * 1024
        ),
        name="dmrg",
    )(left_blocks, right_blocks, start_state, left_transfer, right_transfer, ranks)
    return final[None]


def solution(mesh):
    in_specs = (
        P("seg", "term", None, None),
        P("seg", "term", None, None),
        P("seg", None, None),
        P("seg", None, None),
        P("seg", None, None),
        P("seg", None),
    )
    out_specs = P("seg", None, None)
    return jax.shard_map(
        functools.partial(per_device, mesh.shape["seg"]),
        mesh=mesh, in_specs=in_specs, out_specs=out_specs, check_vma=False,
    )
```

time: 1200 us -> 151 us (0.13)
  waiting for transfers between devices: 883 us -> 0 us
  matrix products: 172 us -> 0 us
  Pallas kernels: 0 us -> 146 us
  other arithmetic: 61.5 us -> 0 us
  local copies, waits for them, and re-layouts: 35.8 us -> 5.3 us
  between operations: 19.3 us -> 0.01 us
  loops' own time: 19.2 us -> 0 us
    all_gather x2 -> x0, waiting for transfers between devices: 460 us -> none  [prefix(): gathered = lax.all_gather(part, axis)]
    psum x4 -> x0, waiting for transfers between devices: 422 us -> none  [half_sweep(): term_total = lax.psum(partial_sum, 'term')]
    dot_general x43 -> x0, matrix products: 172 us -> none  [the longest x31 128 us: combine_env(): jnp.dot(earlier, later, precision=lax.Precision.HIGHEST)]
    pallas_call x0 -> x1, Pallas kernels: none -> 146 us  [per_device(): pl.pallas_call(functools.partial(kernel, nseg, blk, terms), out_shape=jax...]
    mul x34 -> x0, other arithmetic: 38.3 us -> none  [the longest x33 36.8 us: normed(): return block * (target / jnp.sqrt(jnp.sum(block * block) + 1e-06))]
    another operation x2 -> x0, loops' own time: 19.2 us -> none  [prefix(): return lax.fori_loop(0, ahead, one, state)]
    unnamed x30 -> x9, local copies, waits for them, and re-layouts: 21.9 us -> 5.3 us
    reduce_sum x6 -> x0, other arithmetic: 13.2 us -> none  [normed(): return block * (target / jnp.sqrt(jnp.sum(block * block) + 1e-06))]
  transfers between devices with their start and end apart: 7 -> 0, of which waited for: 6 -> 0; matrix products, arithmetic and copies ran while one was open for 16% -> 0% of each run, Pallas kernels for 0% -> 0%
where the time goes in v1:
time: 151 us
  Pallas kernels  146 us (97%)
  local copies, waits for them, and re-layouts  5.3 us (4%)
    pallas_call x1, Pallas kernels, per_device(): pl.pallas_call(functools.partial(kernel, nseg, blk, terms), out_shape=jax...  146 us
    unnamed x9, local copies, waits for them, and re-layouts  5.3 us

profile of v1, /device:TPU:1, one launch (start us, length us, event | category | flops | bytes accessed | tf_op | source)
XLA Modules:
  0.0 151.0 jit_solution(15569543012889526863)
XLA Ops:
  0.0 0.0 copy-start
  0.0 1.2 copy-done
  1.2 0.0 copy-start.1
  1.2 1.2 copy-done.1
  2.5 0.0 copy-start.2
  2.5 1.2 copy-done.2
  3.7 0.0 copy-start.3
  3.7 0.7 copy-done.3
  4.3 145.7 %dmrg.1 = f32[512,512]{1,0:T(8,128)S(1)} custom-call(bf16[1,4,512,512]{3,2,1,0:T(8,128)(2,1)} %left_hbm.1, bf16[1,4,512,512]{3,2,1,0:T(8,128)(2,1)} %right_hbm.1, f32[1,512,512]{2,1,0:T(8,128)S(1)} %copy-done, f32[1,512,512]{2,1,0:T(8,128)S(1)} %copy-done.1, f32[1,512,512]{2,1,0:T(8,128)S(1)} %copy-done.2, s32[1,2]{1,0:T(1,128)S(1)} %copy-done.3), custom_call_target="tpu_custom_call" | custom-call | tf_op jit(solution)/shard_map/dmrg/pallas_call | solution.py:380
  150.0 1.0 copy.8
Async XLA Ops:
  0.0 1.2 copy-start
  1.2 1.2 copy-start.1
  2.5 1.2 copy-start.2
  3.7 0.7 copy-start.3

commit v2 on v1

v2 whole, which is shorter than its diff:
```python
import functools

import jax
import jax.numpy as jnp
from jax import lax
from jax.experimental import pallas as pl
from jax.experimental.pallas import tpu as pltpu
from jax.sharding import PartitionSpec as P

MESH = pl.DeviceIdType.MESH
BF = jnp.bfloat16
F32 = jnp.float32
EPS = 1e-06
ITERS = 2
NY = 4


def dot_ab(a, b):
    return jnp.dot(a, b, preferred_element_type=F32)


def dot_abt(a, b):
    return lax.dot_general(a, b, (((1,), (1,)), ((), ())), preferred_element_type=F32)


def kernel(
    nseg, blk, terms,
    left_hbm, right_hbm, start_hbm, lt_hbm, rt_hbm, ranks_hbm, out_ref,
    ops, ranks, tr, st, unit, hop, link, win, env, env_scale, norms, gath, inner, own, s1_out, s1_in, s2_out, s2_in,
    state, part, state_all, part_all, near_out, near_in,
    in_sem, hop_ss, hop_rs, win_ss, win_rs, norm_ss, norm_rs, early_ss, early_rs, env_ss, env_rs, gath_ss, gath_rs, all_ss, all_rs, sum_ss, sum_rs,
    s1_sem, s2_ss, s2_rs, near_sem,
):
    seg, term = lax.axis_index("seg"), lax.axis_index("term")
    y, core = lax.div(term, 2), lax.rem(term, 2)
    sign = 1 - 2 * core
    place = jnp.where(core == 0, seg, nseg - 1 - seg)
    half, wide, slim = blk // 2, blk // NY, blk // (2 * NY)
    buddy = (seg, term + sign)

    def along(by):
        return (lax.rem(seg + sign * by + nseg, nseg), term)

    def chip(by):
        return (seg, lax.rem(y + by, NY) * 2 + core)

    def rows(index, size):
        return pl.ds(pl.multiple_of(index * size, size), size)

    def remote(src, dst, ss, rs, to):
        return pltpu.make_async_remote_copy(
            src_ref=src, dst_ref=dst, send_sem=ss, recv_sem=rs, device_id=to, device_id_type=MESH
        )

    load_l = pltpu.make_async_copy(left_hbm.at[0], ops.at[0], in_sem.at[0])
    load_r = pltpu.make_async_copy(right_hbm.at[0], ops.at[1], in_sem.at[1])
    load_s = pltpu.make_async_copy(start_hbm.at[0], st, in_sem.at[2])
    load_lt = pltpu.make_async_copy(lt_hbm.at[0], tr, in_sem.at[3])
    load_rt = pltpu.make_async_copy(rt_hbm.at[0], tr, in_sem.at[3])

    @pl.when(core == 0)
    def _():
        load_lt.start()

    @pl.when(core == 1)
    def _():
        load_rt.start()

    load_k = pltpu.make_async_copy(ranks_hbm, ranks, in_sem.at[4])
    load_k.start()
    load_s.start()
    load_l.start()
    load_r.start()

    barrier = pltpu.get_barrier_semaphore()
    sources = [chip(1), chip(2), chip(3), buddy, along(-1), along(-4), along(-8), (lax.rem(seg + nseg - 1, nseg), term)]
    for to in sources:
        pl.semaphore_signal(barrier, inc=1, device_id=to, device_id_type=MESH)
    load_lt.wait()

    root = float(blk) ** 0.5
    at_row = lax.broadcasted_iota(jnp.int32, (slim, blk), 0)
    at_col = lax.broadcasted_iota(jnp.int32, (slim, blk), 1)

    def set_unit(i, _):
        unit[rows(i, slim), :] = tr[rows(i, slim), :].astype(BF)
        return 0

    lax.fori_loop(0, 2 * NY, set_unit, 0)
    pl.semaphore_wait(barrier, len(sources))

    slot = core * NY + y
    my_rows = rows(slot, slim)
    other = rows(1 - core, half)
    ours = rows(core, half)

    def masked(x, low, high):
        live = (at_row + slot * slim < low) & (at_col < high)
        return jnp.where(live, x, 0.0)

    def note(line, x):
        part[pl.ds(line, 1), :] = jnp.broadcast_to(jnp.sum(x * x, axis=(0, 1), keepdims=True), (1, 128))

    def set_start():
        load_s.wait()
        load_k.wait()
        rank0, rank1 = ranks[0, 0], ranks[0, 1]

        def one(i, acc):
            v = st[rows(i, slim), :]
            v = jnp.where((at_row + i * slim < rank0) & (at_col < rank1), v, 0.0)
            st[rows(i, slim), :] = v
            return acc + jnp.sum((v * v).reshape(slim // 8, 8, blk), axis=0)

        acc = lax.fori_loop(0, 2 * NY, one, jnp.zeros((8, blk), F32))
        scale = float(blk) / jnp.sqrt(jnp.sum(acc, axis=(0, 1), keepdims=True) + EPS)
        tr[...] = jnp.transpose(st[...] * scale)
        unit[...] = tr[...].astype(BF)
        state[...] = tr[my_rows, :]
        part[...] = jnp.zeros((8, 128), F32)

    mine = rows(y, wide)

    def gated(distance, x):
        return jnp.where(place < distance, 0.0, x)

    def send_on(j, p, src, by):
        step = remote(src, hop.at[j, p], hop_ss.at[j, p], hop_rs.at[j, p], along(by))
        step.start()
        return step

    def times(j, p, right, distance):
        a = hop[j, p]
        return gated(distance, a.astype(F32) + dot_ab(a, right))

    def my_half(p):
        return rows(2 * y + p, slim)

    steps = [send_on(0, p, unit.at[my_half(p)], 1) for p in range(2)]
    for j in range(3):
        for p in range(2):
            steps[2 * j + p].wait_recv()
            x = (tr[my_half(p), :] + times(j, p, unit[...], 1)).astype(BF)
            if j < 2:
                link[j, p] = x
                steps.append(send_on(j + 1, p, link.at[j, p], 1))
            else:
                win[0, my_half(p), :] = x
    for step in steps:
        step.wait_send()

    for k in range(2):
        w = win.at[k]
        spread = [
            remote(w.at[mine], w.at[mine], win_ss.at[k, i], win_rs.at[k, i], chip(i + 1)) for i in range(3)
        ]
        for i in (1, 0, 2):
            spread[i].start()
        steps = [send_on(3 + k, p, w.at[my_half(p)], 4 << k) for p in range(2)]
        if k == 0:
            set_start()
            base = w[mine, :].astype(F32)
            for i in (None, 0, 2, 1):
                if i is None:
                    for step in steps:
                        step.wait_recv()
                    yy = y
                    acc = jnp.concatenate([hop[3, 0], hop[3, 1]], axis=0).astype(F32)
                else:
                    spread[i].wait_recv()
                    yy = lax.rem(y + NY - 1 - i, NY)
                left = jnp.concatenate([hop[3, p, :, rows(yy, wide)] for p in range(2)], axis=0)
                acc = acc + dot_ab(left, win[k, rows(yy, wide), :])
            win[1, mine, :] = (base + gated(4, acc)).astype(BF)
            for sp in steps:
                sp.wait_send()
        else:
            for i in (0, 2, 1):
                spread[i].wait_recv()
        for sp in spread:
            sp.wait_send()

    for j in range(nseg // 8 - 1):
        by, slot_on = (8, 5 + j) if j < nseg // 8 - 2 else (1, 5 + j)
        for p in range(2):
            steps[2 * j + p].wait_recv()
            x = win[1, my_half(p), :].astype(F32) + times(4 + j, p, win[1], 8)
            link[2 + j, p] = x.astype(BF)
            steps.append(send_on(slot_on, p, link.at[2 + j, p], by))
    for step in steps[-2:]:
        step.wait_recv()
    for step in steps:
        step.wait_send()
    came = jnp.concatenate([hop[3 + nseg // 8, p] for p in range(2)], axis=0)
    at_wide = lax.broadcasted_iota(jnp.int32, (wide, blk), 0) + y * wide
    eye_rows = jnp.where(at_wide == lax.broadcasted_iota(jnp.int32, (wide, blk), 1), 1.0, 0.0)
    rows_f = eye_rows + gated(1, came.astype(F32))
    env[core, mine, :] = rows_f.astype(BF)
    peak = jnp.maximum(jnp.max(jnp.abs(rows_f), axis=(0, 1), keepdims=True), 1e-30)
    scaled = rows_f / peak
    squares = jnp.sum(scaled * scaled, axis=(0, 1), keepdims=True)
    norms[core, y, 0] = jnp.broadcast_to(peak, (8, 128))
    norms[core, y, 1] = jnp.broadcast_to(squares, (8, 128))

    def spread_out(view, ss, rs):
        own_view = view(core, y)
        out = [remote(own_view, own_view, ss.at[i], rs.at[i], chip(i + 1)) for i in range(3)]
        out.append(remote(own_view, own_view, ss.at[3], rs.at[3], buddy))
        for o in out:
            o.start()
        return out

    def pass_on(view, out, ss, rs):
        for i in (0, 2, 1):
            got = view(core, lax.rem(y + NY - 1 - i, NY))
            out[i].wait_recv()
            fwd = remote(got, got, ss.at[4 + i], rs.at[4 + i], buddy)
            fwd.start()
            out.append(fwd)

    def rest(out):
        for o in out[3:]:
            o.wait_recv()

    def sent(out):
        for o in out:
            o.wait_send()

    rank0, rank1 = ranks[0, 0], ranks[0, 1]
    gath_view = lambda c, yy: gath.at[rows(c * NY + yy, slim)]
    all_view = lambda c, yy: state_all.at[rows(c * NY + yy, slim)]
    sum_view = lambda c, yy: part_all.at[c * NY + yy]

    def collect():
        state_all[my_rows, :] = state[...].astype(BF)
        part_all[slot] = part[...]
        sums = spread_out(sum_view, sum_ss, sum_rs)
        full = spread_out(all_view, all_ss, all_rs)
        pass_on(sum_view, sums, sum_ss, sum_rs)
        pass_on(all_view, full, all_ss, all_rs)
        rest(sums)
        rest(full)
        total = part_all[0]
        for i in range(1, 2 * NY):
            total = total + part_all[i]
        sent(sums)
        sent(full)
        return total

    def overall(total, scale):
        for line in range(1, ITERS + 1):
            s = total[line : line + 1, 0:1]
            scale = scale * (float(blk) / jnp.sqrt(scale * scale * s + EPS))
        return scale

    def turn():
        @pl.when(core == 0)
        def _():
            env_from_buddy()

        total = collect()
        scale = overall(total, jnp.ones((1, 1), F32))
        pick = jnp.where(at_row + slot * slim == at_col, 1.0, 0.0).astype(BF)
        first = dot_abt(pick, state_all[...]) * scale
        near_out[...] = first.astype(BF)
        to = (lax.rem(seg + 1, nseg), term)
        step = remote(near_out, near_in, near_sem.at[0], near_sem.at[1], to)
        step.start()
        step.wait()
        near = jnp.where(seg > 0, near_in[...].astype(F32), 0.0)
        x = masked(first + 0.5 * near, rank0, rank1)
        state[...] = x
        note(0, x)

    def apply_first(at, h, gain):
        for w in range(terms):
            inner[w, at, :] = (dot_abt(gath[at, :], ops[h, w]) * gain).astype(BF)

    def apply_second(at, h):
        acc = dot_ab(ops[1 - h, 0, at, :], inner[0])
        for w in range(1, terms):
            acc = acc + dot_ab(ops[1 - h, w, at, :], inner[w])
        return acc

    def add_up(h, out, late):
        s1_out[...] = apply_second(other, h).astype(BF)
        pair = remote(s1_out, s1_in, s1_sem.at[0], s1_sem.at[1], buddy)
        pair.start()
        own[...] = apply_second(ours, h)
        sent(out)
        pair.wait_recv()
        pieces = [None] * 3
        for i in (1, 0, 2):
            to = rows(lax.rem(y + 1 + i, NY), slim)
            s2_out[i] = (own[to, :] + s1_in[to, :].astype(F32)).astype(BF)
            pieces[i] = remote(s2_out.at[i], s2_in.at[i], s2_ss.at[i], s2_rs.at[i], chip(i + 1))
            pieces[i].start()
        total = own[rows(y, slim), :] + s1_in[rows(y, slim), :].astype(F32)
        late()
        for i in (0, 2, 1):
            pieces[i].wait_recv()
            total = total + s2_in[i].astype(F32)
        pair.wait_send()
        for piece in pieces:
            piece.wait_send()
        return total.astype(BF)

    def advance(line, applied, gain, live_row, live_col):
        x = masked(2.0 * state[...] - applied * gain, live_row, live_col)
        state[...] = x
        note(line, x)

    cols = lambda yy: gath.at[:, rows(yy, wide)]
    norm_view = lambda c, yy: norms.at[c, yy]
    env_view = lambda c, yy: env.at[c, rows(yy, wide)]

    def early(i):
        block = cols(y) if i < 4 else cols(lax.rem(y + NY - 1 - (i - 4), NY))
        to = chip(i + 1) if i < 3 else buddy
        return remote(block, block, early_ss.at[i], early_rs.at[i], to)

    def env_copy(i):
        block = env_view(core, y if i < 4 else lax.rem(y + NY - 1 - (i - 4), NY))
        return remote(block, block, env_ss.at[i], env_rs.at[i], chip(i + 1) if i < 3 else buddy)

    def env_pass_on():
        for i in (0, 2, 1):
            env_copy(i).wait_recv()
            env_copy(4 + i).start()

    def env_from_buddy():
        for i in range(3, 7):
            block = env_view(1 - core, y if i < 4 else lax.rem(y + NY - 1 - (i - 4), NY))
            remote(block, block, env_ss.at[i], env_rs.at[i], buddy).wait_recv()

    def spread_env():
        @pl.when(core == 0)
        def _():
            env_pass_on()

        @pl.when(core == 1)
        def _():
            for i in range(4):
                env_copy(i).start()

    @pl.when(core == 0)
    def _():
        gath[:, mine] = dot_abt(unit[...], env[0, mine, :]).astype(BF)
        for i in range(4):
            early(i).start()
        for i in range(4):
            env_copy(i).start()

    norm_out = spread_out(norm_view, norm_ss, norm_rs)
    pass_on(norm_view, norm_out, norm_ss, norm_rs)

    @pl.when(core == 0)
    def _():
        for i in (0, 2, 1):
            come = cols(lax.rem(y + NY - 1 - i, NY))
            remote(come, come, early_ss.at[i], early_rs.at[i], chip(i + 1)).wait_recv()
            early(4 + i).start()

    rest(norm_out)
    for h in range(2):
        peaks = [norms[h, i, 0, 0:1, 0:1] for i in range(NY)]
        top = functools.reduce(jnp.maximum, peaks)
        whole = jnp.zeros((1, 1), F32)
        for i in range(NY):
            ratio = peaks[i] / top
            whole = whole + norms[h, i, 1, 0:1, 0:1] * (ratio * ratio)
        env_scale[h] = jnp.broadcast_to(root / (top * jnp.sqrt(whole + EPS)), (8, 128))

    @pl.when(core == 1)
    def _():
        for i in range(3, 7):
            come = cols(y) if i < 4 else cols(lax.rem(y + NY - 1 - (i - 4), NY))
            remote(come, come, early_ss.at[i], early_rs.at[i], buddy).wait_recv()

    load_l.wait()
    gain = env_scale[0, 0:1, 0:1]
    apply_first(ours, 0, gain)
    apply_first(other, 0, gain)

    @pl.when(core == 0)
    def _():
        for i in range(7):
            early(i).wait_send()

    load_r.wait()
    total = add_up(0, norm_out, spread_env)

    @pl.when(core == 1)
    def _():
        env_from_buddy()

    advance(1, dot_ab(total, env[0]), gain, rank1, rank0)

    def iteration(n, _):
        h = lax.div(n, ITERS)
        gain = env_scale[h, 0:1, 0:1]

        @pl.when(n == ITERS)
        def _():
            turn()

        x = state[...].astype(BF)

        @pl.when(h == 0)
        def _():
            gath[my_rows, :] = (dot_abt(x, env[0]) * gain).astype(BF)

        @pl.when(h == 1)
        def _():
            gath[my_rows, :] = (dot_ab(x, env[1]) * gain).astype(BF)

        out = spread_out(gath_view, gath_ss, gath_rs)
        pass_on(gath_view, out, gath_ss, gath_rs)
        apply_first(ours, h, 1.0)
        rest(out)
        apply_first(other, h, 1.0)
        total = add_up(h, out, lambda: None)

        @pl.when(h == 0)
        def _():
            advance(1 + n, dot_ab(total, env[0]), gain, rank1, rank0)

            @pl.when(core == 1)
            def _():
                env_pass_on()

        @pl.when(h == 1)
        def _():
            advance(1 + n - ITERS, dot_abt(total, env[1]), gain, rank0, rank1)

        return 0

    lax.fori_loop(1, 2 * ITERS, iteration, 0)
    for i in range(7):
        env_copy(i).wait_send()
    total = collect()
    scale = overall(total, float(blk) / jnp.sqrt(total[0:1, 0:1] + EPS))
    out_ref[...] = state_all[...].astype(F32) * scale


def per_device(nseg, left_blocks, right_blocks, start_state, left_transfer, right_transfer, ranks):
    blk, terms = left_blocks.shape[-1], left_blocks.shape[1]
    half, wide, slim = blk // 2, blk // NY, blk // (2 * NY)
    dma = pltpu.SemaphoreType.DMA
    scratch = [
        pltpu.VMEM((2, terms, blk, blk), BF),
        pltpu.SMEM((1, 2), jnp.int32),
        pltpu.VMEM((blk, blk), F32),
        pltpu.VMEM((blk, blk), F32),
        pltpu.VMEM((blk, blk), BF),
        pltpu.VMEM((4 + nseg // 8, 2, slim, blk), BF),
        pltpu.VMEM((1 + nseg // 8, 2, slim, blk), BF),
        pltpu.VMEM((2, blk, blk), BF),
        pltpu.VMEM((2, blk, blk), BF),
        pltpu.VMEM((2, 8, 128), F32),
        pltpu.VMEM((2, NY, 2, 8, 128), F32),
        pltpu.VMEM((blk, blk), BF),
        pltpu.VMEM((terms, blk, blk), BF),
        pltpu.VMEM((half, blk), F32),
        pltpu.VMEM((half, blk), BF),
        pltpu.VMEM((half, blk), BF),
        pltpu.VMEM((3, slim, blk), BF),
        pltpu.VMEM((3, slim, blk), BF),
        pltpu.VMEM((slim, blk), F32),
        pltpu.VMEM((8, 128), F32),
        pltpu.VMEM((blk, blk), BF),
        pltpu.VMEM((2 * NY, 8, 128), F32),
        pltpu.VMEM((slim, blk), BF),
        pltpu.VMEM((slim, blk), BF),
        dma((5,)),
        dma((4 + nseg // 8, 2)), dma((4 + nseg // 8, 2)),
        dma((2, 3)), dma((2, 3)),
        dma((7,)), dma((7,)),
        dma((7,)), dma((7,)),
        dma((7,)), dma((7,)),
        dma((7,)), dma((7,)),
        dma((7,)), dma((7,)),
        dma((7,)), dma((7,)),
        dma((2,)),
        dma((3,)), dma((3,)),
        dma((2,)),
    ]
    hbm = pl.BlockSpec(memory_space=pltpu.HBM)
    final = pl.pallas_call(
        functools.partial(kernel, nseg, blk, terms),
        out_shape=jax.ShapeDtypeStruct((blk, blk), F32),
        in_specs=[hbm] * 6,
        out_specs=pl.BlockSpec(memory_space=pltpu.VMEM),
        scratch_shapes=scratch,
        compiler_params=pltpu.CompilerParams(
            collective_id=0, has_side_effects=True, vmem_limit_bytes=52 * 1024 * 1024
        ),
        name="dmrg",
    )(left_blocks, right_blocks, start_state, left_transfer, right_transfer, ranks)
    return final[None]


def solution(mesh):
    in_specs = (
        P("seg", "term", None, None),
        P("seg", "term", None, None),
        P("seg", None, None),
        P("seg", None, None),
        P("seg", None, None),
        P("seg", None),
    )
    out_specs = P("seg", None, None)
    return jax.shard_map(
        functools.partial(per_device, mesh.shape["seg"]),
        mesh=mesh, in_specs=in_specs, out_specs=out_specs, check_vma=False,
    )
```

time: 151 us -> 134 us (0.89)
  Pallas kernels: 146 us -> 132 us
  local copies, waits for them, and re-layouts: 5.3 us -> 1.63 us
    pallas_call x1, Pallas kernels: 146 us -> 132 us  [per_device(): pl.pallas_call(functools.partial(kernel, nseg, blk, terms), out_shape=jax...]
    unnamed x9 -> x3, local copies, waits for them, and re-layouts: 5.3 us -> 1.63 us
where the time goes in v2:
time: 134 us
  Pallas kernels  132 us (99%)
  local copies, waits for them, and re-layouts  1.63 us (1%)
    pallas_call x1, Pallas kernels, per_device(): pl.pallas_call(functools.partial(kernel, nseg, blk, terms), out_shape=jax...  132 us

profile of v2, /device:TPU:1, one launch (start us, length us, event | category | flops | bytes accessed | tf_op | source)
XLA Modules:
  0.0 133.6 jit_solution(12947868762204909403)
XLA Ops:
  0.0 0.0 copy-start
  0.0 0.7 copy-done
  0.7 132.0 %dmrg.1 = f32[512,512]{1,0:T(8,128)S(1)} custom-call(bf16[1,4,512,512]{3,2,1,0:T(8,128)(2,1)} %left_hbm.1, bf16[1,4,512,512]{3,2,1,0:T(8,128)(2,1)} %right_hbm.1, f32[1,512,512]{2,1,0:T(8,128)} %start_hbm.1, f32[1,512,512]{2,1,0:T(8,128)} %lt_hbm.1, f32[1,512,512]{2,1,0:T(8,128)} %rt_hbm.1, s32[1,2]{1,0:T(1,128)S(1)} %copy-done), custom_call_target="tpu_custom_call" | custom-call | tf_op jit(solution)/shard_map/dmrg/pallas_call | solution.py:489
  132.6 1.0 copy.8
Async XLA Ops:
  0.0 0.7 copy-start

commit v3 on v2

--- a/solution.py
+++ b/solution.py
@@ -27,9 +27,9 @@
     nseg, blk, terms,
     left_hbm, right_hbm, start_hbm, lt_hbm, rt_hbm, ranks_hbm, out_ref,
     ops, ranks, tr, st, unit, hop, link, win, env, env_scale, norms, gath, inner, own, s1_out, s1_in, s2_out, s2_in,
-    state, part, state_all, part_all, near_out, near_in,
+    state, part, state_all, part_all, turned, swap_out, swap_in, placing,
     in_sem, hop_ss, hop_rs, win_ss, win_rs, norm_ss, norm_rs, early_ss, early_rs, env_ss, env_rs, gath_ss, gath_rs, all_ss, all_rs, sum_ss, sum_rs,
-    s1_sem, s2_ss, s2_rs, near_sem,
+    s1_sem, s2_ss, s2_rs, swap_ss, swap_rs,
 ):
     seg, term = lax.axis_index("seg"), lax.axis_index("term")
     y, core = lax.div(term, 2), lax.rem(term, 2)
@@ -73,7 +73,7 @@
     load_r.start()
 
     barrier = pltpu.get_barrier_semaphore()
-    sources = [chip(1), chip(2), chip(3), buddy, along(-1), along(-4), along(-8), (lax.rem(seg + nseg - 1, nseg), term)]
+    sources = [chip(1), chip(2), chip(3), buddy, along(-1), along(-4), along(-8)]
     for to in sources:
         pl.semaphore_signal(barrier, inc=1, device_id=to, device_id_type=MESH)
     load_lt.wait()
@@ -118,6 +118,11 @@
         unit[...] = tr[...].astype(BF)
         state[...] = tr[my_rows, :]
         part[...] = jnp.zeros((8, 128), F32)
+        turned[...] = jnp.zeros_like(turned)
+        for q in range(2 * NY):
+            at = lax.broadcasted_iota(jnp.int32, (2 * slim, blk), 0)
+            to = lax.broadcasted_iota(jnp.int32, (2 * slim, blk), 1) - q * slim
+            placing[q * 2 * slim : (q + 1) * 2 * slim, :] = jnp.where((at == to) & (at < slim), 1.0, 0.0).astype(BF)
 
     mine = rows(y, wide)
 
@@ -258,19 +263,53 @@
         def _():
             env_from_buddy()
 
-        total = collect()
-        scale = overall(total, jnp.ones((1, 1), F32))
-        pick = jnp.where(at_row + slot * slim == at_col, 1.0, 0.0).astype(BF)
-        first = dot_abt(pick, state_all[...]) * scale
-        near_out[...] = first.astype(BF)
-        to = (lax.rem(seg + 1, nseg), term)
-        step = remote(near_out, near_in, near_sem.at[0], near_sem.at[1], to)
-        step.start()
-        step.wait()
-        near = jnp.where(seg > 0, near_in[...].astype(F32), 0.0)
-        x = masked(first + 0.5 * near, rank0, rank1)
+        turned[0:slim, :] = state[...]
+        for line in range(1, ITERS + 1):
+            v = part[line : line + 1, 0:1]
+            high = v.astype(BF).astype(F32)
+            mid = (v - high).astype(BF).astype(F32)
+            for j, piece in enumerate((high, mid, v - high - mid)):
+                at = slim + 3 * (line - 1) + j
+                turned[at : at + 1, :] = jnp.broadcast_to(piece, (1, blk))
+        swap_out[...] = jnp.transpose(turned[...]).astype(BF)
+        copies = []
+        for there in (1, 0):
+            for i in range(2 * NY):
+                dy, dc = i // 2, i % 2
+                if there or i:
+                    to_y, to_core = lax.rem(y + dy, NY), core if dc == 0 else 1 - core
+                    to = (lax.rem(seg + there, nseg), to_y * 2 + to_core)
+                    at = 2 * NY * there + i
+                    copy = remote(
+                        swap_out.at[rows(to_core * NY + to_y, slim)], swap_in.at[there, slot],
+                        swap_ss.at[at], swap_rs.at[at], to,
+                    )
+                    copy.start()
+                    copies.append(copy)
+        swap_in[0, slot] = swap_out[my_rows, :]
+        for copy in copies:
+            copy.wait_recv()
+        wide_rows = [jnp.concatenate([swap_in[g, q] for q in range(2 * NY)], axis=1) for g in range(2)]
+        both = dot_ab(jnp.concatenate(wide_rows, axis=0), placing[...])
+        lane = lax.broadcasted_iota(jnp.int32, (1, 2 * slim), 1)
+
+        def seen(g):
+            sums = swap_in[g, 0, 0:16, :].astype(F32)
+            for q in range(1, 2 * NY):
+                sums = sums + swap_in[g, q, 0:16, :].astype(F32)
+            scale = jnp.ones((1, 1), F32)
+            for line in range(1, ITERS + 1):
+                at = slim + 3 * (line - 1)
+                s = jnp.sum(jnp.where((lane >= at) & (lane < at + 3), sums[0:1, :], 0.0), axis=(0, 1), keepdims=True)
+                scale = scale * (float(blk) / jnp.sqrt(scale * scale * s + EPS))
+            return both[g * slim : (g + 1) * slim] * scale
+
+        near = jnp.where(seg > 0, seen(1).astype(BF).astype(F32), 0.0)
+        x = masked(seen(0) + 0.5 * near, rank0, rank1)
         state[...] = x
         note(0, x)
+        for copy in copies:
+            copy.wait_send()
 
     def apply_first(at, h, gain):
         for w in range(terms):
@@ -470,8 +509,10 @@
         pltpu.VMEM((8, 128), F32),
         pltpu.VMEM((blk, blk), BF),
         pltpu.VMEM((2 * NY, 8, 128), F32),
-        pltpu.VMEM((slim, blk), BF),
-        pltpu.VMEM((slim, blk), BF),
+        pltpu.VMEM((2 * slim, blk), F32),
+        pltpu.VMEM((blk, 2 * slim), BF),
+        pltpu.VMEM((2, 2 * NY, slim, 2 * slim), BF),
+        pltpu.VMEM((2 * blk, blk), BF),
         dma((5,)),
         dma((4 + nseg // 8, 2)), dma((4 + nseg // 8, 2)),
         dma((2, 3)), dma((2, 3)),
@@ -483,7 +524,7 @@
         dma((7,)), dma((7,)),
         dma((2,)),
         dma((3,)), dma((3,)),
-        dma((2,)),
+        dma((4 * NY,)), dma((4 * NY,)),
     ]
     hbm = pl.BlockSpec(memory_space=pltpu.HBM)
     final = pl.pallas_call(

time: 134 us -> 130 us (0.970)
  Pallas kernels: 132 us -> 128 us
    pallas_call x1, Pallas kernels: 132 us -> 128 us  [per_device(): pl.pallas_call(functools.partial(kernel, nseg, blk, terms), out_shape=jax...]
where the time goes in v3:
time: 130 us
  Pallas kernels  128 us (98%)
  local copies, waits for them, and re-layouts  1.63 us (1%)
    pallas_call x1, Pallas kernels, per_device(): pl.pallas_call(functools.partial(kernel, nseg, blk, terms), out_shape=jax...  128 us

profile of v3, /device:TPU:1, one launch (start us, length us, event | category | flops | bytes accessed | tf_op | source)
XLA Modules:
  0.0 129.6 jit_solution(11899712249613373465)
XLA Ops:
  0.0 0.0 copy-start
  0.0 0.7 copy-done
  0.7 128.0 %dmrg.1 = f32[512,512]{1,0:T(8,128)S(1)} custom-call(bf16[1,4,512,512]{3,2,1,0:T(8,128)(2,1)} %left_hbm.1, bf16[1,4,512,512]{3,2,1,0:T(8,128)(2,1)} %right_hbm.1, f32[1,512,512]{2,1,0:T(8,128)} %start_hbm.1, f32[1,512,512]{2,1,0:T(8,128)} %lt_hbm.1, f32[1,512,512]{2,1,0:T(8,128)} %rt_hbm.1, s32[1,2]{1,0:T(1,128)S(1)} %copy-done), custom_call_target="tpu_custom_call" | custom-call | tf_op jit(solution)/shard_map/dmrg/pallas_call | solution.py:530
  128.6 1.0 copy.8
Async XLA Ops:
  0.0 0.7 copy-start

commit v4 on v3

--- a/solution.py
+++ b/solution.py
@@ -13,6 +13,7 @@
 EPS = 1e-06
 ITERS = 2
 NY = 4
+PIECES = 4
 
 
 def dot_ab(a, b):
@@ -66,16 +67,17 @@
     def _():
         load_rt.start()
 
+    barrier = pltpu.get_barrier_semaphore()
+    sources = [chip(1), chip(2), chip(3), buddy, along(-1), along(-4), along(-8)]
+    for to in sources:
+        pl.semaphore_signal(barrier, inc=1, device_id=to, device_id_type=MESH)
+
     load_k = pltpu.make_async_copy(ranks_hbm, ranks, in_sem.at[4])
     load_k.start()
     load_s.start()
     load_l.start()
     load_r.start()
 
-    barrier = pltpu.get_barrier_semaphore()
-    sources = [chip(1), chip(2), chip(3), buddy, along(-1), along(-4), along(-8)]
-    for to in sources:
-        pl.semaphore_signal(barrier, inc=1, device_id=to, device_id_type=MESH)
     load_lt.wait()
 
     root = float(blk) ** 0.5
@@ -138,19 +140,19 @@
         a = hop[j, p]
         return gated(distance, a.astype(F32) + dot_ab(a, right))
 
-    def my_half(p):
-        return rows(2 * y + p, slim)
-
-    steps = [send_on(0, p, unit.at[my_half(p)], 1) for p in range(2)]
+    def my_piece(p):
+        return rows(PIECES * y + p, wide // PIECES)
+
+    steps = [send_on(0, p, unit.at[my_piece(p)], 1) for p in range(PIECES)]
     for j in range(3):
-        for p in range(2):
-            steps[2 * j + p].wait_recv()
-            x = (tr[my_half(p), :] + times(j, p, unit[...], 1)).astype(BF)
+        for p in range(PIECES):
+            steps[PIECES * j + p].wait_recv()
+            x = (tr[my_piece(p), :] + times(j, p, unit[...], 1)).astype(BF)
             if j < 2:
                 link[j, p] = x
                 steps.append(send_on(j + 1, p, link.at[j, p], 1))
             else:
-                win[0, my_half(p), :] = x
+                win[0, my_piece(p), :] = x
     for step in steps:
         step.wait_send()
 
@@ -161,7 +163,7 @@
         ]
         for i in (1, 0, 2):
             spread[i].start()
-        steps = [send_on(3 + k, p, w.at[my_half(p)], 4 << k) for p in range(2)]
+        steps = [send_on(3 + k, p, w.at[my_piece(p)], 4 << k) for p in range(PIECES)]
         if k == 0:
             set_start()
             base = w[mine, :].astype(F32)
@@ -170,11 +172,11 @@
                     for step in steps:
                         step.wait_recv()
                     yy = y
-                    acc = jnp.concatenate([hop[3, 0], hop[3, 1]], axis=0).astype(F32)
+                    acc = jnp.concatenate([hop[3, p] for p in range(PIECES)], axis=0).astype(F32)
                 else:
                     spread[i].wait_recv()
                     yy = lax.rem(y + NY - 1 - i, NY)
-                left = jnp.concatenate([hop[3, p, :, rows(yy, wide)] for p in range(2)], axis=0)
+                left = jnp.concatenate([hop[3, p, :, rows(yy, wide)] for p in range(PIECES)], axis=0)
                 acc = acc + dot_ab(left, win[k, rows(yy, wide), :])
             win[1, mine, :] = (base + gated(4, acc)).astype(BF)
             for sp in steps:
@@ -187,16 +189,16 @@
 
     for j in range(nseg // 8 - 1):
         by, slot_on = (8, 5 + j) if j < nseg // 8 - 2 else (1, 5 + j)
-        for p in range(2):
-            steps[2 * j + p].wait_recv()
-            x = win[1, my_half(p), :].astype(F32) + times(4 + j, p, win[1], 8)
+        for p in range(PIECES):
+            steps[PIECES * j + p].wait_recv()
+            x = win[1, my_piece(p), :].astype(F32) + times(4 + j, p, win[1], 8)
             link[2 + j, p] = x.astype(BF)
             steps.append(send_on(slot_on, p, link.at[2 + j, p], by))
-    for step in steps[-2:]:
+    for step in steps[-PIECES:]:
         step.wait_recv()
     for step in steps:
         step.wait_send()
-    came = jnp.concatenate([hop[3 + nseg // 8, p] for p in range(2)], axis=0)
+    came = jnp.concatenate([hop[3 + nseg // 8, p] for p in range(PIECES)], axis=0)
     at_wide = lax.broadcasted_iota(jnp.int32, (wide, blk), 0) + y * wide
     eye_rows = jnp.where(at_wide == lax.broadcasted_iota(jnp.int32, (wide, blk), 1), 1.0, 0.0)
     rows_f = eye_rows + gated(1, came.astype(F32))
@@ -377,18 +379,11 @@
         def _():
             env_pass_on()
 
-        @pl.when(core == 1)
-        def _():
-            for i in range(4):
-                env_copy(i).start()
-
     @pl.when(core == 0)
     def _():
         gath[:, mine] = dot_abt(unit[...], env[0, mine, :]).astype(BF)
         for i in range(4):
             early(i).start()
-        for i in range(4):
-            env_copy(i).start()
 
     norm_out = spread_out(norm_view, norm_ss, norm_rs)
     pass_on(norm_view, norm_out, norm_ss, norm_rs)
@@ -399,6 +394,8 @@
             come = cols(lax.rem(y + NY - 1 - i, NY))
             remote(come, come, early_ss.at[i], early_rs.at[i], chip(i + 1)).wait_recv()
             early(4 + i).start()
+        for i in range(4):
+            env_copy(i).start()
 
     rest(norm_out)
     for h in range(2):
@@ -455,6 +452,12 @@
 
         out = spread_out(gath_view, gath_ss, gath_rs)
         pass_on(gath_view, out, gath_ss, gath_rs)
+
+        @pl.when((n == 1) & (core == 1))
+        def _():
+            for i in range(4):
+                env_copy(i).start()
+
         apply_first(ours, h, 1.0)
         rest(out)
         apply_first(other, h, 1.0)
@@ -492,8 +495,8 @@
         pltpu.VMEM((blk, blk), F32),
         pltpu.VMEM((blk, blk), F32),
         pltpu.VMEM((blk, blk), BF),
-        pltpu.VMEM((4 + nseg // 8, 2, slim, blk), BF),
-        pltpu.VMEM((1 + nseg // 8, 2, slim, blk), BF),
+        pltpu.VMEM((4 + nseg // 8, PIECES, wide // PIECES, blk), BF),
+        pltpu.VMEM((1 + nseg // 8, PIECES, wide // PIECES, blk), BF),
         pltpu.VMEM((2, blk, blk), BF),
         pltpu.VMEM((2, blk, blk), BF),
         pltpu.VMEM((2, 8, 128), F32),
@@ -514,7 +517,7 @@
         pltpu.VMEM((2, 2 * NY, slim, 2 * slim), BF),
         pltpu.VMEM((2 * blk, blk), BF),
         dma((5,)),
-        dma((4 + nseg // 8, 2)), dma((4 + nseg // 8, 2)),
+        dma((4 + nseg // 8, PIECES)), dma((4 + nseg // 8, PIECES)),
         dma((2, 3)), dma((2, 3)),
         dma((7,)), dma((7,)),
         dma((7,)), dma((7,)),

time: 130 us -> 125 us (0.962)
  Pallas kernels: 128 us -> 123 us
    pallas_call x1, Pallas kernels: 128 us -> 123 us  [per_device(): pl.pallas_call(functools.partial(kernel, nseg, blk, terms), out_shape=jax...]
where the time goes in v4:
time: 125 us
  Pallas kernels  123 us (98%)
  local copies, waits for them, and re-layouts  1.63 us (1%)
    pallas_call x1, Pallas kernels, per_device(): pl.pallas_call(functools.partial(kernel, nseg, blk, terms), out_shape=jax...  123 us

profile of v4, /device:TPU:1, one launch (start us, length us, event | category | flops | bytes accessed | tf_op | source)
XLA Modules:
  0.0 124.7 jit_solution(12416240794339972751)
XLA Ops:
  0.0 0.0 copy-start
  0.0 0.7 copy-done
  0.7 123.0 %dmrg.1 = f32[512,512]{1,0:T(8,128)S(1)} custom-call(bf16[1,4,512,512]{3,2,1,0:T(8,128)(2,1)} %left_hbm.1, bf16[1,4,512,512]{3,2,1,0:T(8,128)(2,1)} %right_hbm.1, f32[1,512,512]{2,1,0:T(8,128)} %start_hbm.1, f32[1,512,512]{2,1,0:T(8,128)} %lt_hbm.1, f32[1,512,512]{2,1,0:T(8,128)} %rt_hbm.1, s32[1,2]{1,0:T(1,128)S(1)} %copy-done), custom_call_target="tpu_custom_call" | custom-call | tf_op jit(solution)/shard_map/dmrg/pallas_call | solution.py:533
  123.7 1.0 copy.8
Async XLA Ops:
  0.0 0.7 copy-start

commit v5 on v4

--- a/solution.py
+++ b/solution.py
@@ -30,7 +30,7 @@
     ops, ranks, tr, st, unit, hop, link, win, env, env_scale, norms, gath, inner, own, s1_out, s1_in, s2_out, s2_in,
     state, part, state_all, part_all, turned, swap_out, swap_in, placing,
     in_sem, hop_ss, hop_rs, win_ss, win_rs, norm_ss, norm_rs, early_ss, early_rs, env_ss, env_rs, gath_ss, gath_rs, all_ss, all_rs, sum_ss, sum_rs,
-    s1_sem, s2_ss, s2_rs, swap_ss, swap_rs,
+    s1_sem, s2_ss, s2_rs, swap_ss, swap_rs, go,
 ):
     seg, term = lax.axis_index("seg"), lax.axis_index("term")
     y, core = lax.div(term, 2), lax.rem(term, 2)
@@ -73,12 +73,10 @@
         pl.semaphore_signal(barrier, inc=1, device_id=to, device_id_type=MESH)
 
     load_k = pltpu.make_async_copy(ranks_hbm, ranks, in_sem.at[4])
-    load_k.start()
-    load_s.start()
-    load_l.start()
-    load_r.start()
 
     load_lt.wait()
+    for load in (load_k, load_s, load_l, load_r):
+        load.start()
 
     root = float(blk) ** 0.5
     at_row = lax.broadcasted_iota(jnp.int32, (slim, blk), 0)
@@ -88,7 +86,6 @@
         unit[rows(i, slim), :] = tr[rows(i, slim), :].astype(BF)
         return 0
 
-    lax.fori_loop(0, 2 * NY, set_unit, 0)
     pl.semaphore_wait(barrier, len(sources))
 
     slot = core * NY + y
@@ -143,21 +140,30 @@
     def my_piece(p):
         return rows(PIECES * y + p, wide // PIECES)
 
-    steps = [send_on(0, p, unit.at[my_piece(p)], 1) for p in range(PIECES)]
+    for p in range(PIECES):
+        link[0, p] = tr[my_piece(p), :].astype(BF)
+    steps = [send_on(0, p, link.at[0, p], 1) for p in range(PIECES)]
+    lax.fori_loop(0, 2 * NY, set_unit, 0)
     for j in range(3):
         for p in range(PIECES):
             steps[PIECES * j + p].wait_recv()
             x = (tr[my_piece(p), :] + times(j, p, unit[...], 1)).astype(BF)
             if j < 2:
-                link[j, p] = x
-                steps.append(send_on(j + 1, p, link.at[j, p], 1))
+                link[1 + j, p] = x
+                steps.append(send_on(j + 1, p, link.at[1 + j, p], 1))
             else:
                 win[0, my_piece(p), :] = x
     for step in steps:
         step.wait_send()
 
+    def let_go():
+        @pl.when(core == 0)
+        def _():
+            pl.semaphore_signal(go, inc=1, device_id=buddy, device_id_type=MESH)
+
     for k in range(2):
         w = win.at[k]
+
         spread = [
             remote(w.at[mine], w.at[mine], win_ss.at[k, i], win_rs.at[k, i], chip(i + 1)) for i in range(3)
         ]
@@ -192,8 +198,8 @@
         for p in range(PIECES):
             steps[PIECES * j + p].wait_recv()
             x = win[1, my_piece(p), :].astype(F32) + times(4 + j, p, win[1], 8)
-            link[2 + j, p] = x.astype(BF)
-            steps.append(send_on(slot_on, p, link.at[2 + j, p], by))
+            link[3 + j, p] = x.astype(BF)
+            steps.append(send_on(slot_on, p, link.at[3 + j, p], by))
     for step in steps[-PIECES:]:
         step.wait_recv()
     for step in steps:
@@ -213,8 +219,8 @@
         own_view = view(core, y)
         out = [remote(own_view, own_view, ss.at[i], rs.at[i], chip(i + 1)) for i in range(3)]
         out.append(remote(own_view, own_view, ss.at[3], rs.at[3], buddy))
-        for o in out:
-            o.start()
+        for i in (1, 0, 2, 3):
+            out[i].start()
         return out
 
     def pass_on(view, out, ss, rs):
@@ -241,10 +247,10 @@
     def collect():
         state_all[my_rows, :] = state[...].astype(BF)
         part_all[slot] = part[...]
+        full = spread_out(all_view, all_ss, all_rs)
         sums = spread_out(sum_view, sum_ss, sum_rs)
-        full = spread_out(all_view, all_ss, all_rs)
+        pass_on(all_view, full, all_ss, all_rs)
         pass_on(sum_view, sums, sum_ss, sum_rs)
-        pass_on(all_view, full, all_ss, all_rs)
         rest(sums)
         rest(full)
         total = part_all[0]
@@ -263,7 +269,10 @@
     def turn():
         @pl.when(core == 0)
         def _():
-            env_from_buddy()
+            env_arrive()
+            norm_arrive()
+
+        set_scale(1)
 
         turned[0:slim, :] = state[...]
         for line in range(1, ITERS + 1):
@@ -355,50 +364,36 @@
     norm_view = lambda c, yy: norms.at[c, yy]
     env_view = lambda c, yy: env.at[c, rows(yy, wide)]
 
-    def early(i):
-        block = cols(y) if i < 4 else cols(lax.rem(y + NY - 1 - (i - 4), NY))
-        to = chip(i + 1) if i < 3 else buddy
-        return remote(block, block, early_ss.at[i], early_rs.at[i], to)
-
-    def env_copy(i):
-        block = env_view(core, y if i < 4 else lax.rem(y + NY - 1 - (i - 4), NY))
-        return remote(block, block, env_ss.at[i], env_rs.at[i], chip(i + 1) if i < 3 else buddy)
-
-    def env_pass_on():
-        for i in (0, 2, 1):
-            env_copy(i).wait_recv()
-            env_copy(4 + i).start()
-
-    def env_from_buddy():
-        for i in range(3, 7):
-            block = env_view(1 - core, y if i < 4 else lax.rem(y + NY - 1 - (i - 4), NY))
-            remote(block, block, env_ss.at[i], env_rs.at[i], buddy).wait_recv()
-
-    def spread_env():
-        @pl.when(core == 0)
-        def _():
-            env_pass_on()
-
-    @pl.when(core == 0)
-    def _():
-        gath[:, mine] = dot_abt(unit[...], env[0, mine, :]).astype(BF)
-        for i in range(4):
-            early(i).start()
-
-    norm_out = spread_out(norm_view, norm_ss, norm_rs)
-    pass_on(norm_view, norm_out, norm_ss, norm_rs)
-
-    @pl.when(core == 0)
-    def _():
-        for i in (0, 2, 1):
-            come = cols(lax.rem(y + NY - 1 - i, NY))
-            remote(come, come, early_ss.at[i], early_rs.at[i], chip(i + 1)).wait_recv()
-            early(4 + i).start()
-        for i in range(4):
-            env_copy(i).start()
-
-    rest(norm_out)
-    for h in range(2):
+    def from_this_core(view, ss, rs):
+        def copy(i):
+            block = view(core, y if i < 4 else lax.rem(y + NY - 1 - (i - 4), NY))
+            return remote(block, block, ss.at[i], rs.at[i], chip(i + 1) if i < 3 else buddy)
+
+        def start():
+            for i in (1, 0, 2, 3):
+                copy(i).start()
+
+        def forward():
+            for i in (0, 2, 1):
+                copy(i).wait_recv()
+                copy(4 + i).start()
+
+        def arrive():
+            for i in range(3, 7):
+                block = view(1 - core, y if i < 4 else lax.rem(y + NY - 1 - (i - 4), NY))
+                remote(block, block, ss.at[i], rs.at[i], buddy).wait_recv()
+
+        def finish():
+            for i in range(7):
+                copy(i).wait_send()
+
+        return start, forward, arrive, finish
+
+    norm_start, norm_forward, norm_arrive, norm_finish = from_this_core(norm_view, norm_ss, norm_rs)
+    env_start, env_forward, env_arrive, env_finish = from_this_core(env_view, env_ss, env_rs)
+    col_start, col_forward, col_arrive, col_finish = from_this_core(lambda c, yy: cols(yy), early_ss, early_rs)
+
+    def set_scale(h):
         peaks = [norms[h, i, 0, 0:1, 0:1] for i in range(NY)]
         top = functools.reduce(jnp.maximum, peaks)
         whole = jnp.zeros((1, 1), F32)
@@ -407,12 +402,26 @@
             whole = whole + norms[h, i, 1, 0:1, 0:1] * (ratio * ratio)
         env_scale[h] = jnp.broadcast_to(root / (top * jnp.sqrt(whole + EPS)), (8, 128))
 
+    def spread_env():
+        @pl.when(core == 0)
+        def _():
+            env_forward()
+
+    @pl.when(core == 0)
+    def _():
+        gath[:, mine] = dot_abt(unit[...], env[0, mine, :]).astype(BF)
+        col_start()
+        norm_start()
+        col_forward()
+        norm_forward()
+        env_start()
+
     @pl.when(core == 1)
     def _():
-        for i in range(3, 7):
-            come = cols(y) if i < 4 else cols(lax.rem(y + NY - 1 - (i - 4), NY))
-            remote(come, come, early_ss.at[i], early_rs.at[i], buddy).wait_recv()
-
+        norm_arrive()
+        col_arrive()
+
+    set_scale(0)
     load_l.wait()
     gain = env_scale[0, 0:1, 0:1]
     apply_first(ours, 0, gain)
@@ -420,26 +429,25 @@
 
     @pl.when(core == 0)
     def _():
-        for i in range(7):
-            early(i).wait_send()
+        col_finish()
 
     load_r.wait()
-    total = add_up(0, norm_out, spread_env)
+    total = add_up(0, [], spread_env)
 
     @pl.when(core == 1)
     def _():
-        env_from_buddy()
+        env_arrive()
 
     advance(1, dot_ab(total, env[0]), gain, rank1, rank0)
 
     def iteration(n, _):
         h = lax.div(n, ITERS)
+
+        @pl.when(n == ITERS)
+        def _():
+            turn()
+
         gain = env_scale[h, 0:1, 0:1]
-
-        @pl.when(n == ITERS)
-        def _():
-            turn()
-
         x = state[...].astype(BF)
 
         @pl.when(h == 0)
@@ -455,8 +463,8 @@
 
         @pl.when((n == 1) & (core == 1))
         def _():
-            for i in range(4):
-                env_copy(i).start()
+            env_start()
+            norm_start()
 
         apply_first(ours, h, 1.0)
         rest(out)
@@ -469,7 +477,8 @@
 
             @pl.when(core == 1)
             def _():
-                env_pass_on()
+                env_forward()
+                norm_forward()
 
         @pl.when(h == 1)
         def _():
@@ -478,8 +487,8 @@
         return 0
 
     lax.fori_loop(1, 2 * ITERS, iteration, 0)
-    for i in range(7):
-        env_copy(i).wait_send()
+    env_finish()
+    norm_finish()
     total = collect()
     scale = overall(total, float(blk) / jnp.sqrt(total[0:1, 0:1] + EPS))
     out_ref[...] = state_all[...].astype(F32) * scale
@@ -496,7 +505,7 @@
         pltpu.VMEM((blk, blk), F32),
         pltpu.VMEM((blk, blk), BF),
         pltpu.VMEM((4 + nseg // 8, PIECES, wide // PIECES, blk), BF),
-        pltpu.VMEM((1 + nseg // 8, PIECES, wide // PIECES, blk), BF),
+        pltpu.VMEM((2 + nseg // 8, PIECES, wide // PIECES, blk), BF),
         pltpu.VMEM((2, blk, blk), BF),
         pltpu.VMEM((2, blk, blk), BF),
         pltpu.VMEM((2, 8, 128), F32),
@@ -528,6 +537,7 @@
         dma((2,)),
         dma((3,)), dma((3,)),
         dma((4 * NY,)), dma((4 * NY,)),
+        pltpu.SemaphoreType.REGULAR,
     ]
     hbm = pl.BlockSpec(memory_space=pltpu.HBM)
     final = pl.pallas_call(

time: 125 us -> 124 us (level)
  no operation moved by 1% of the time
where the time goes in v5:
time: 124 us
  Pallas kernels  123 us (99%)
  local copies, waits for them, and re-layouts  1.63 us (1%)
    pallas_call x1, Pallas kernels, per_device(): pl.pallas_call(functools.partial(kernel, nseg, blk, terms), out_shape=jax...  123 us

profile of v5, /device:TPU:1, one launch (start us, length us, event | category | flops | bytes accessed | tf_op | source)
XLA Modules:
  0.0 124.2 jit_solution(11805358265606749031)
XLA Ops:
  0.0 0.0 copy-start
  0.0 0.7 copy-done
  0.7 122.5 %dmrg.1 = f32[512,512]{1,0:T(8,128)S(1)} custom-call(bf16[1,4,512,512]{3,2,1,0:T(8,128)(2,1)} %left_hbm.1, bf16[1,4,512,512]{3,2,1,0:T(8,128)(2,1)} %right_hbm.1, f32[1,512,512]{2,1,0:T(8,128)} %start_hbm.1, f32[1,512,512]{2,1,0:T(8,128)} %lt_hbm.1, f32[1,512,512]{2,1,0:T(8,128)} %rt_hbm.1, s32[1,2]{1,0:T(1,128)S(1)} %copy-done), custom_call_target="tpu_custom_call" | custom-call | tf_op jit(solution)/shard_map/dmrg/pallas_call | solution.py:543
  123.2 1.0 copy.8
Async XLA Ops:
  0.0 0.7 copy-start

commit v6 on v5

--- a/solution.py
+++ b/solution.py
@@ -267,12 +267,6 @@
         return scale
 
     def turn():
-        @pl.when(core == 0)
-        def _():
-            env_arrive()
-            norm_arrive()
-
-        set_scale(1)
 
         turned[0:slim, :] = state[...]
         for line in range(1, ITERS + 1):
@@ -298,6 +292,13 @@
                     copy.start()
                     copies.append(copy)
         swap_in[0, slot] = swap_out[my_rows, :]
+
+        @pl.when(core == 0)
+        def _():
+            env_arrive()
+            norm_arrive()
+
+        set_scale(1)
         for copy in copies:
             copy.wait_recv()
         wide_rows = [jnp.concatenate([swap_in[g, q] for q in range(2 * NY)], axis=1) for g in range(2)]
@@ -410,18 +411,25 @@
     @pl.when(core == 0)
     def _():
         gath[:, mine] = dot_abt(unit[...], env[0, mine, :]).astype(BF)
+        norm_start()
         col_start()
-        norm_start()
+        norm_forward()
+
+    @pl.when(core == 1)
+    def _():
+        norm_arrive()
+
+    set_scale(0)
+
+    @pl.when(core == 0)
+    def _():
         col_forward()
-        norm_forward()
         env_start()
 
     @pl.when(core == 1)
     def _():
-        norm_arrive()
         col_arrive()
 
-    set_scale(0)
     load_l.wait()
     gain = env_scale[0, 0:1, 0:1]
     apply_first(ours, 0, gain)

time: 124 us -> 123 us (level)
  no operation moved by 1% of the time
where the time goes in v6:
time: 123 us
  Pallas kernels  122 us (99%)
  local copies, waits for them, and re-layouts  1.63 us (1%)
    pallas_call x1, Pallas kernels, per_device(): pl.pallas_call(functools.partial(kernel, nseg, blk, terms), out_shape=jax...  122 us

profile of v6, /device:TPU:1, one launch (start us, length us, event | category | flops | bytes accessed | tf_op | source)
XLA Modules:
  0.0 123.4 jit_solution(13941245314795002678)
XLA Ops:
  0.0 0.0 copy-start
  0.0 0.7 copy-done
  0.7 121.7 %dmrg.1 = f32[512,512]{1,0:T(8,128)S(1)} custom-call(bf16[1,4,512,512]{3,2,1,0:T(8,128)(2,1)} %left_hbm.1, bf16[1,4,512,512]{3,2,1,0:T(8,128)(2,1)} %right_hbm.1, f32[1,512,512]{2,1,0:T(8,128)} %start_hbm.1, f32[1,512,512]{2,1,0:T(8,128)} %lt_hbm.1, f32[1,512,512]{2,1,0:T(8,128)} %rt_hbm.1, s32[1,2]{1,0:T(1,128)S(1)} %copy-done), custom_call_target="tpu_custom_call" | custom-call | tf_op jit(solution)/shard_map/dmrg/pallas_call | solution.py:551
  122.4 1.0 copy.8
Async XLA Ops:
  0.0 0.7 copy-start
